TPU v7x, 256 devices: a whole 4x4x8 slice. The times are simulated.
256 devices in a mesh: bin: 64 (over x, z, core), line: 4 (over y).
Axes of the slice: x: 4, y: 4, z: 8, core: 2. Of those that a mesh axis runs over, the one named last changes fastest.
Arguments:
- traces: float32 [4, 16384, 1024], P('line', 'bin'), may hold values from -6 to 6
- trace_cell: int32 [4, 16384], P('line', 'bin'), may hold values from 0 to 4095, as said below
- pattern: int32 [4, 16384], P('line', 'bin'), may hold values from 0 to 15
- fold: int32 [16, 1024], P('line', 'bin'), may hold values from 1 to 40, as said below
Outputs:
- spectrum: float32 [1024, 16, 1024], P('bin', 'line')
Inputs may be any that keep to these rules, and one draw needn't show every extreme that they name: `trace_cell`: the traces held by one device lie in the bins of one index of bin at most 8 times, and that count is reached; the bins of each index of bin receive exactly 256 traces of each line group. fold[l, j] is the number of traces whose cell is (l, j); it reaches 40.
All inputs are finite; a program needn't handle non-finite values.
Results may differ from a plain program's by a relative error of at most 0.0001.
Values sent between devices are 32-bit elements; how exact they have to be, the bound alone decides.
A program may use at most 192 MiB of HBM per device.

v0:
```python
import math

import jax
import jax.numpy as jnp
from jax import lax
from jax.sharding import PartitionSpec as P

RADIUS = 2
PATTERNS = 16


def extended(block, sides, width):
    for axis, dim in sides:
        count = lax.axis_size(axis)
        forward = [(i, i + 1) for i in range(count - 1)]
        backward = [(target, source) for source, target in forward]
        low = lax.ppermute(
            lax.slice_in_dim(block, block.shape[dim] - width, None, axis=dim), axis, forward
        )
        high = lax.ppermute(lax.slice_in_dim(block, 0, width, axis=dim), axis, backward)
        block = jnp.concatenate([low, block, high], axis=dim)
    return block


def sinc_table():
    shifts = jnp.arange(-RADIUS, RADIUS + 1).astype(jnp.float32)
    offsets = (jnp.arange(PATTERNS).astype(jnp.float32) + 0.5) / PATTERNS - 0.5
    spread = shifts[:, None] - offsets[None, :]
    return jnp.sinc(spread) * jnp.cos(jnp.pi * spread / (2 * RADIUS + 2)) ** 2


def dft_table(length):
    times = jnp.arange(length, dtype=jnp.int32)
    freqs = jnp.arange(length // 2, dtype=jnp.int32)
    phase = 2.0 * jnp.pi * (times[:, None] * freqs[None, :] % length).astype(jnp.float32) / length
    scale = 1.0 / math.sqrt(length)
    return jnp.concatenate([jnp.cos(phase), -jnp.sin(phase)], axis=1) * scale


def lookup(weights, pattern_ids):
    picker = (pattern_ids[None, :] == jnp.arange(PATTERNS, dtype=jnp.int32)[:, None]).astype(
        jnp.float32
    )
    return jnp.dot(weights, picker, precision=lax.Precision.HIGHEST)


def per_device(traces, trace_cell, pattern, fold):
    records = traces[0]
    bin_count = lax.axis_size("bin")
    lines_dev, bins_dev = fold.shape
    total_bins = bins_dev * bin_count
    length = records.shape[1]
    spectral = dft_table(length)
    weights = sinc_table()
    stencil = 2 * RADIUS + 1
    cell_ids = trace_cell[0]
    pattern_ids = pattern[0]
    record_count = records.shape[0]
    capacity = 2 * record_count // bin_count
    target = cell_ids % total_bins // bins_dev
    local_cell = cell_ids // total_bins * bins_dev + cell_ids % bins_dev
    onehot = (target[:, None] == jnp.arange(bin_count, dtype=jnp.int32)[None, :]).astype(jnp.int32)
    position = jnp.sum(jnp.cumsum(onehot, axis=0) * onehot, axis=1) - 1
    slot_index = target * capacity + position
    outgoing = jnp.zeros((bin_count * capacity, length), jnp.float32).at[slot_index].set(records)
    labels = (
        jnp.full((bin_count * capacity,), -1, jnp.int32)
        .at[slot_index]
        .set(local_cell * PATTERNS + pattern_ids)
    )
    arrived, arrived_tags = (
        lax.all_to_all(outgoing, "bin", split_axis=0, concat_axis=0, tiled=True),
        lax.all_to_all(labels, "bin", split_axis=0, concat_axis=0, tiled=True),
    )
    owned = arrived_tags // PATTERNS
    factors = lookup(weights, arrived_tags % PATTERNS)
    select = (owned[None, :] == jnp.arange(lines_dev * bins_dev, dtype=jnp.int32)[:, None]).astype(
        jnp.float32
    )
    mixing = (factors[:, None, :] * select[None]).reshape(stencil * lines_dev * bins_dev, -1)
    stacked = jnp.dot(mixing, arrived, precision=lax.Precision.HIGHEST).reshape(
        stencil, lines_dev, bins_dev, length
    )
    padded = extended(stacked, (("line", 1),), RADIUS)
    regular = jnp.zeros((lines_dev, bins_dev, length), jnp.float32)
    for offset in range(stencil):
        regular = regular + padded[offset, 2 * RADIUS - offset : 2 * RADIUS - offset + lines_dev]
    regular = regular / fold.astype(jnp.float32)[:, :, None]
    flattened = regular.reshape(lines_dev * bins_dev, length)
    spectrum = lax.dot_general(
        spectral, flattened, (((0,), (1,)), ((), ())), precision=lax.Precision.HIGHEST
    )
    spectrum = spectrum.reshape(-1, lines_dev, bins_dev)
    return lax.all_to_all(spectrum, "bin", split_axis=0, concat_axis=2, tiled=True)


def solution(mesh):
    return jax.shard_map(
        per_device,
        mesh=mesh,
        in_specs=(P("line", "bin", None), P("line", "bin"), P("line", "bin"), P("line", "bin")),
        out_specs=P("bin", "line", None),
        check_vma=False,
    )
```

profile of v0, /device:TPU:1, one launch (start us, length us, event | category | flops | bytes accessed | tf_op | source)
XLA Modules:
  0.0 143.9 jit_solution(7525116436438542451)
XLA Ops:
  3.2 1.4 scatter_custom_fusion
  5.3 13.0 %all-to-all-start = ((s32[64,8,1]{1,2,0:T(1,128)}), s32[64,8,1]{1,2,0:T(1,128)S(1)}, u32[]{:S(2)}, u32[]{:S(2)}) async-start(s32[64,8,1]{1,2,0:T(1,128)} %bitcast.8), calls=%async_computation | async-start | bytes 65536 | tf_op jit(solution)/shard_map/all_to_all | solution.py:73
  18.3 2.9 %scatter_custom_fusion.1 = f32[512,1024]{1,0:T(8,128)} fusion(s32[256]{0:T(256)S(1)} %bitcast.66, f32[1,256,1024]{2,1,0:T(8,128)S(1)} %copy-done, f32[]{:T(128)} %constant.128.clone.1), kind=kCustom, calls=%fused_computation.21 | custom fusion | bytes 3145732 | tf_op jit(solution)/shard_map/scatter | solution.py:65
  21.2 6.3 %all-to-all-done = s32[64,8,1]{1,2,0:T(1,128)S(1)} async-done(((s32[64,8,1]{1,2,0:T(1,128)}), s32[64,8,1]{1,2,0:T(1,128)S(1)}, u32[]{:S(2)}, u32[]{:S(2)}) %all-to-all-start) | async-done | bytes 2080 | tf_op jit(solution)/shard_map/all_to_all | solution.py:73
  27.5 4.8 %all-to-all-start.1 = ((f32[64,8,1024]{2,1,0:T(8,128)}), f32[64,8,1024]{2,1,0:T(8,128)S(1)}, u32[]{:S(2)}, u32[]{:S(2)}) async-start(f32[64,8,1024]{2,1,0:T(8,128)} %bitcast.11), calls=%async_computation.1 | async-start | bytes 4194304 | tf_op jit(solution)/shard_map/all_to_all | solution.py:72
  33.9 0.9 broadcast_multiply_fusion
  34.8 48.8 %all-to-all-done.1 = f32[64,8,1024]{2,1,0:T(8,128)S(1)} async-done(((f32[64,8,1024]{2,1,0:T(8,128)}), f32[64,8,1024]{2,1,0:T(8,128)S(1)}, u32[]{:S(2)}, u32[]{:S(2)}) %all-to-all-start.1) | async-done | bytes 2097184 | tf_op jit(solution)/shard_map/all_to_all | solution.py:72
  83.7 1.3 copy-done.1
  85.0 4.1 %fusion.8 = f32[320,1024]{1,0:T(8,128)S(1)} fusion(f32[320,512]{1,0:T(8,128)} %bitcast.60, f32[64,8,1024]{2,1,0:T(8,128)} %copy-done.1), kind=kOutput, calls=%fused_computation.14 | convolution fusion | flops 2013265920 | bytes 4063232 | tf_op jit(solution)/shard_map/dot_general | solution.py:81
  89.1 1.0 fusion.98
  90.1 1.3 collective-permute-start
  91.4 4.9 %collective-permute-start.1 = (f32[5,2,16,1024]{3,2,1,0:T(8,128)S(1)}, f32[5,2,16,1024]{3,2,1,0:T(8,128)}, u32[]{:S(2)}, u32[]{:S(2)}) collective-permute-start(f32[5,2,16,1024]{3,2,1,0:T(8,128)S(1)} %get-tuple-element.9), channel_id=1, source_target_pairs={{0,1},{1,2},{2,3},{4,5},{5,6},{6,7},{8,9},{9,10},{10,11},{12,13},{... | collective-permute-start | bytes 1966088 | tf_op jit(solution)/shard_map/ppermute | solution.py:17
  96.3 8.2 %sine_negate_fusion = (f32[1024,512]{1,0:T(8,128)S(1)}, f32[1024,512]{1,0:T(8,128)S(1)}) fusion(), kind=kLoop, calls=%fused_computation.17 | loop fusion | flops 7864320 | bytes 4194304 | tf_op jit(solution)/shard_map/neg | solution.py:37
  104.6 3.6 %collective-permute-done = f32[5,2,16,1024]{3,2,1,0:T(8,128)} collective-permute-done((f32[5,2,16,1024]{3,2,1,0:T(8,128)}, f32[5,2,16,1024]{3,2,1,0:T(8,128)}, u32[]{:S(2)}, u32[]{:S(2)}) %collective-permute-start) | collective-permute-done | bytes 655392 | tf_op jit(solution)/shard_map/ppermute | solution.py:20
  108.8 1.1 pad_maximum_fusion.1
  109.9 2.8 %fusion.1 = f32[1024,4,16]{0,2,1:T(8,128)S(1)} fusion(f32[4,16,1024]{2,1,0:T(8,128)S(1)} %bitcast.61, f32[1024,512]{1,0:T(8,128)S(1)} %get-tuple-element.14, f32[1024,512]{1,0:T(8,128)S(1)} %get-tuple-element.15), kind=kOutput, calls=%fused_computation.4 | convolution fusion | flops 807403520 | bytes 4718592 | tf_op jit(solution)/shard_map/dot_general | solution.py:90
  112.8 1.1 copy.11
  113.9 1.6 %reshape.296 = f32[64,1,1024]{2,1,0:T(1,128)S(1)} reshape(f32[1024,4,16]{2,1,0:T(4,128)S(1)} %copy.11) | data formatting | bytes 524288
  115.4 18.6 %all_to_all.42 = f32[64,1,1024]{2,1,0:T(1,128)S(1)} all-to-all(f32[64,1,1024]{2,1,0:T(1,128)S(1)} %reshape.296), channel_id=1, replica_groups=mesh['bin'=64,'line'=4] {'bin'}, dimensions={0} | all-to-all | bytes 524288 | tf_op jit(solution)/shard_map/all_to_all | solution.py:94
  134.5 1.3 reduce.6
  135.8 1.5 %reshape.297 = f32[1024,4,16]{2,1,0:T(4,128)S(1)} reshape(f32[64,1024]{1,0:T(8,128)S(1)} %reduce.6) | data formatting | bytes 524288
  137.3 2.6 %copy.20 = f32[64,16,4,16]{3,0,1,2:T(8,128)} copy(f32[64,16,4,16]{3,2,1,0:T(4,128)S(1)} %bitcast.58) | data formatting | bytes 524288 | tf_op jit(solution)/shard_map/all_to_all | solution.py:94
  139.9 3.1 %all_to_all.38 = f32[16,4,1024]{2,0,1:T(8,128)S(1)} reshape(f32[16,4,64,16]{3,2,0,1:T(8,128)} %bitcast.59) | data formatting | bytes 524288 | tf_op jit(solution)/shard_map/all_to_all | solution.py:94
  143.0 0.9 copy.14
  (29 shorter events, 6.7 us)
Async XLA Ops:
  0.0 18.3 %copy-start = (f32[1,256,1024]{2,1,0:T(8,128)S(1)}, f32[1,256,1024]{2,1,0:T(8,128)}, u32[]{:S(2)}) copy-start(f32[1,256,1024]{2,1,0:T(8,128)} %param.4) | copy-start | bytes 3145732
  5.3 22.2 %all-to-all-start = ((s32[64,8,1]{1,2,0:T(1,128)}), s32[64,8,1]{1,2,0:T(1,128)S(1)}, u32[]{:S(2)}, u32[]{:S(2)}) async-start(s32[64,8,1]{1,2,0:T(1,128)} %bitcast.8), calls=%async_computation | async-start | bytes 65536 | tf_op jit(solution)/shard_map/all_to_all | solution.py:73
  27.5 56.2 %all-to-all-start.1 = ((f32[64,8,1024]{2,1,0:T(8,128)}), f32[64,8,1024]{2,1,0:T(8,128)S(1)}, u32[]{:S(2)}, u32[]{:S(2)}) async-start(f32[64,8,1024]{2,1,0:T(8,128)} %bitcast.11), calls=%async_computation.1 | async-start | bytes 4194304 | tf_op jit(solution)/shard_map/all_to_all | solution.py:72
  83.7 1.4 copy-start.1
  89.1 7.1 %copy-start.2 = (s32[4,16]{1,0:T(4,128)S(1)}, s32[4,16]{1,0:T(4,128)}, u32[]{:S(2)}) copy-start(s32[4,16]{1,0:T(4,128)} %param.7) | copy-start | bytes 772
  90.1 18.1 %collective-permute-start = (f32[5,2,16,1024]{3,2,1,0:T(8,128)}, f32[5,2,16,1024]{3,2,1,0:T(8,128)}, u32[]{:S(2)}, u32[]{:S(2)}) collective-permute-start(f32[5,2,16,1024]{3,2,1,0:T(8,128)} %get-tuple-element.8), channel_id=1, source_target_pairs={{1,0},{2,1},{3,2},{5,4},{6,5},{7,6},{9,8},{10,9},{11,10},{13,12},{... | collective-permute-start | bytes 1966088 | tf_op jit(solution)/shard_map/ppermute | solution.py:20
  91.4 17.4 %collective-permute-start.1 = (f32[5,2,16,1024]{3,2,1,0:T(8,128)S(1)}, f32[5,2,16,1024]{3,2,1,0:T(8,128)}, u32[]{:S(2)}, u32[]{:S(2)}) collective-permute-start(f32[5,2,16,1024]{3,2,1,0:T(8,128)S(1)} %get-tuple-element.9), channel_id=1, source_target_pairs={{0,1},{1,2},{2,3},{4,5},{5,6},{6,7},{8,9},{9,10},{10,11},{12,13},{... | collective-permute-start | bytes 1966088 | tf_op jit(solution)/shard_map/ppermute | solution.py:17
where the time goes:
time: 146 us; the launch traced here: 144 us
  waiting for transfers between devices  59.3 us (41%)
  starting transfers between devices  23.9 us (16%)
  local copies, waits for them, and re-layouts  19.4 us (13%)
  blocking collectives  18.6 us (13%)
  other arithmetic  15.3 us (10%)
  matrix products  7.19 us (5%)
    all_to_all x1, waiting for transfers between devices, per_device(): lax.all_to_all(outgoing, 'bin', split_axis=0, concat_axis=0, tiled=True)  48.8 us
    all_to_all x1, blocking collectives, per_device(): lax.all_to_all(spectrum, 'bin', split_axis=0, concat_axis=2, tiled=True)  18.6 us
    all_to_all x1, starting transfers between devices, per_device(): lax.all_to_all(labels, 'bin', split_axis=0, concat_axis=0, tiled=True)  13 us
    neg x1, other arithmetic, dft_table(): return jnp.concatenate([jnp.cos(phase), -jnp.sin(phase)], axis=1) * scale  8.24 us
    all_to_all x4, local copies, waits for them, and re-layouts, per_device(): lax.all_to_all(spectrum, 'bin', split_axis=0, concat_axis=2, tiled=True)  7.09 us
    all_to_all x1, waiting for transfers between devices, per_device(): lax.all_to_all(labels, 'bin', split_axis=0, concat_axis=0, tiled=True)  6.28 us
    ppermute x1, starting transfers between devices, extended(): lax.ppermute(lax.slice_in_dim(block, block.shape[dim] - width, None, axis...  4.85 us
    all_to_all x1, starting transfers between devices, per_device(): lax.all_to_all(outgoing, 'bin', split_axis=0, concat_axis=0, tiled=True)  4.79 us
  transfers between devices with their start and end apart: 4, of which 4 were waited for; matrix products, arithmetic and copies ran while one was open for 10% of the time, Pallas kernels for 0%

commit v1 on v0

v1 whole, which is shorter than its diff:
```python
import functools
import math

import jax
import jax.numpy as jnp
import numpy as np
from jax import lax
from jax.experimental import pallas as pl
from jax.experimental.pallas import tpu as pltpu
from jax.sharding import PartitionSpec as P

RADIUS = 2
PATTERNS = 16
NX, NZ, NC, NY = 4, 8, 2, 4
N_BIN = NX * NZ * NC
LANES = 128
GROUP = 4
NT_DOT = (((1,), (1,)), ((), ()))
MESH = pl.DeviceIdType.MESH


def sinc_table():
    shifts = np.arange(-RADIUS, RADIUS + 1)
    offsets = (np.arange(PATTERNS) + 0.5) / PATTERNS - 0.5
    spread = shifts[:, None] - offsets[None, :]
    table = np.zeros((8, LANES), np.float32)
    table[: 2 * RADIUS + 1, :PATTERNS] = (
        np.sinc(spread) * np.cos(np.pi * spread / (2 * RADIUS + 2)) ** 2
    )
    return table


def dft_tables(length):
    times = np.arange(length)
    freqs = np.arange(length // 2)
    phase = 2.0 * np.pi * (freqs[:, None] * times[None, :] % length) / length
    full = np.concatenate([np.cos(phase), -np.sin(phase)], axis=0) / math.sqrt(length)
    high = full.astype(jnp.bfloat16)
    low = (full - high.astype(np.float64)).astype(jnp.bfloat16)
    return high, low


def split(values):
    high = values.astype(jnp.bfloat16)
    return high, (values - high.astype(jnp.float32)).astype(jnp.bfloat16)


def dot_nt(a, b):
    return lax.dot_general(a, b, NT_DOT, preferred_element_type=jnp.float32)


def place():
    b = lax.axis_index("bin")
    return b // (NZ * NC), b // NC % NZ, b % NC, lax.axis_index("line")


def device(x, z, c):
    return (x * NZ + z) * NC + c


def kernel(
    traces_hbm, cell_ref, pattern_ref, fold_ref, high_hbm, low_hbm, sinc_ref,
    out_ref,
    traces, high, low, spec, recv, meta, folds, fold_sum, acc, onehot, mixed, halo,
    load_sem, meta_ssem, meta_rsem, fold_ssem, fold_rsem, send_sem, recv_sem, halo_ssem, halo_rsem,
):
    bins = acc.shape[1]
    x, z, c, y = place()
    me = device(x, z, c)

    def along_z(k):
        return device(x, (z + k) % NZ, c)

    def across(k):
        return device((x + k // NC) % NX, z, (c + k) % NC)

    loads = [
        pltpu.make_async_copy(src, dst, load_sem.at[i])
        for i, (src, dst) in enumerate(((traces_hbm, traces), (high_hbm, high), (low_hbm, low)))
    ]
    for load in loads:
        load.start()

    barrier = pltpu.get_barrier_semaphore()
    for k in range(1, NZ):
        pl.semaphore_signal(barrier, inc=1, device_id=(along_z(k), y), device_id_type=MESH)
    for k in range(1, NX * NC):
        pl.semaphore_signal(barrier, inc=1, device_id=(across(k), y), device_id_type=MESH)
    above, below = (y + 1) % NY, (y + NY - 1) % NY
    for other in (above, below):
        pl.semaphore_signal(barrier, inc=1, device_id=(me, other), device_id_type=MESH)

    for i in range(2):
        meta[0, 0, pl.ds(i, 1), :] = cell_ref[:, pl.ds(i * LANES, LANES)]
        meta[0, 0, pl.ds(2 + i, 1), :] = pattern_ref[:, pl.ds(i * LANES, LANES)]
    lanes = fold_ref.shape[1]
    spread_row = lax.broadcasted_iota(jnp.int32, (lanes, LANES), 0)
    spread_lane = lax.broadcasted_iota(jnp.int32, (lanes, LANES), 1)
    spread = (spread_lane == (z % 4) * (NC * lanes) + c * lanes + spread_row).astype(jnp.float32)
    fold_row = jnp.dot(
        fold_ref[...].astype(jnp.float32), spread, preferred_element_type=jnp.float32
    )
    fold_both = jnp.concatenate([fold_row, fold_row], axis=0)
    half = lax.broadcasted_iota(jnp.int32, fold_both.shape, 0) // 4
    folds[0] = jnp.where(half == z // 4, fold_both, 0.0)

    for load in loads:
        load.wait()
    t_high, t_low = split(traces[...])

    def transform(i, carry):
        rows = pl.ds(pl.multiple_of(i * 256, 256), 256)
        f_high = high[rows, :]
        spec[rows, :] = (
            dot_nt(f_high, t_low) + dot_nt(low[rows, :], t_high) + dot_nt(f_high, t_high)
        )
        return carry

    lax.fori_loop(0, spec.shape[0] // 256, transform, 0)

    pl.semaphore_wait(barrier, NZ - 1 + NX * NC - 1 + 2)

    first = []
    for k in range(1, NZ):
        first.append(pltpu.make_async_remote_copy(
            meta.at[0, 0], meta.at[0, k], meta_ssem.at[k], meta_rsem.at[k],
            device_id=(along_z(k), y), device_id_type=MESH))
        first.append(pltpu.make_async_remote_copy(
            folds.at[0], folds.at[k], fold_ssem.at[k], fold_rsem.at[k],
            device_id=(along_z(k), y), device_id_type=MESH))
    for copy in first:
        copy.start()
    for copy in first:
        copy.wait_recv()
    fold_sum[0] = jnp.sum(folds[...], axis=0)
    second = []
    for k in range(1, NX * NC):
        second.append(pltpu.make_async_remote_copy(
            meta.at[0], meta.at[k], meta_ssem.at[NZ + k], meta_rsem.at[NZ + k],
            device_id=(across(k), y), device_id_type=MESH))
        second.append(pltpu.make_async_remote_copy(
            fold_sum.at[0], fold_sum.at[k], fold_ssem.at[NZ + k], fold_rsem.at[NZ + k],
            device_id=(across(k), y), device_id_type=MESH))
    for copy in second:
        copy.start()
    for copy in second:
        copy.wait_recv()

    slice_rows = recv.shape[1]

    def sent(k):
        a, d = k // NZ, k % NZ
        target = device((x + a // NC) % NX, (z + d) % NZ, (c + a) % NC)
        return pltpu.make_async_remote_copy(
            spec.at[pl.ds(pl.multiple_of(target * slice_rows, slice_rows), slice_rows)],
            recv.at[k], send_sem.at[k], recv_sem.at[k],
            device_id=(target, y), device_id_type=MESH)

    def start_one(k, carry):
        sent(k).start()
        return carry

    lax.fori_loop(1, N_BIN, start_one, 0)
    recv[0] = spec[pl.ds(pl.multiple_of(me * slice_rows, slice_rows), slice_rows), :]

    acc[...] = jnp.zeros_like(acc)
    records = recv.shape[2]

    def stack(i, carry):
        for j in range(GROUP):
            k = i * GROUP + j

            @pl.when(k > 0)
            def _():
                sent(k).wait_recv()

            tags = meta[k // NZ, k % NZ]
            cell = jnp.concatenate([tags[0:1], tags[1:2]], axis=1)
            pattern = jnp.broadcast_to(
                jnp.concatenate([tags[2:3], tags[3:4]], axis=1), (8, records)
            )
            taps = jnp.zeros((8, records), jnp.float32)
            for q in range(PATTERNS):
                taps = jnp.where(pattern == q, sinc_ref[:, q : q + 1], taps)
            line = jnp.broadcast_to(cell // bins, (8, records))
            weights = taps
            for s in range(1, 4):
                weights = jnp.where(line == s, pltpu.roll(taps, s, 0), weights)
            terms = (weights[:, None, :] * recv[k][None, :, :]).reshape(8 * slice_rows, records)
            t_high, t_low = split(terms)
            columns = pl.ds(j * records, records)
            mixed[pl.ds(0, 8 * slice_rows), columns] = t_high
            mixed[pl.ds(8 * slice_rows, 8 * slice_rows), columns] = t_low
            where = cell % bins
            for g in range(0, bins, 256):
                row = lax.broadcasted_iota(jnp.int32, (256, records), 0) + g
                onehot[pl.ds(g, 256), columns] = (
                    (row == jnp.broadcast_to(where, (256, records)))
                    .astype(jnp.float32)
                    .astype(jnp.bfloat16)
                )
        for g in range(0, bins, 256):
            acc[:, pl.ds(g, 256)] += dot_nt(mixed[...], onehot[pl.ds(g, 256), :])
        return carry

    lax.fori_loop(0, N_BIN // GROUP, stack, 0)

    full = 8 * slice_rows
    edge = 2 * slice_rows
    halo[0] = acc[pl.ds(0, edge), :] + acc[pl.ds(full, edge), :]
    halo[1] = acc[pl.ds(full - edge, edge), :] + acc[pl.ds(2 * full - edge, edge), :]
    down = pltpu.make_async_remote_copy(
        halo.at[0], halo.at[2], halo_ssem.at[0], halo_rsem.at[0],
        device_id=(me, below), device_id_type=MESH)
    up = pltpu.make_async_remote_copy(
        halo.at[1], halo.at[3], halo_ssem.at[1], halo_rsem.at[1],
        device_id=(me, above), device_id_type=MESH)
    down.start()
    up.start()
    counts = []
    for i in range(NX):
        block = None
        for j in range(NC):
            slot = (x + NX - i) % NX * NC + j
            part = fold_sum[slot]
            block = part if block is None else block + part
        counts.append(block)
    inverse = 1.0 / jnp.concatenate(
        [block[4 * h : 4 * h + 4] for block in counts for h in range(2)], axis=1
    )
    down.wait()
    up.wait()
    for line in range(4):
        rows = pl.ds((line + 2) * slice_rows, slice_rows)
        low_rows = pl.ds(full + (line + 2) * slice_rows, slice_rows)
        value = acc[rows, :] + acc[low_rows, :]
        if line < 2:
            extra = halo[3, pl.ds(line * slice_rows, slice_rows), :]
            inside = y > 0
        else:
            extra = halo[2, pl.ds((line - 2) * slice_rows, slice_rows), :]
            inside = y < NY - 1
        value = value + jnp.where(inside, extra, 0.0)
        out_ref[:, line, :] = value * inverse[line : line + 1, :]

    for copy in first + second:
        copy.wait_send()

    def finish_one(k, carry):
        sent(k).wait_send()
        return carry

    lax.fori_loop(1, N_BIN, finish_one, 0)


def per_device(traces, trace_cell, pattern, fold):
    _, records, length = traces.shape
    lines, bins_dev = fold.shape
    bins = bins_dev * N_BIN
    rows = length // N_BIN
    high, low = dft_tables(length)
    anywhere = pl.BlockSpec(memory_space=pl.ANY)
    vmem = pl.BlockSpec(memory_space=pltpu.VMEM)
    f32, i32, bf16 = jnp.float32, jnp.int32, jnp.bfloat16
    return pl.pallas_call(
        kernel,
        out_shape=jax.ShapeDtypeStruct((rows, lines, bins), f32),
        in_specs=[anywhere, vmem, vmem, vmem, anywhere, anywhere, vmem],
        out_specs=vmem,
        scratch_shapes=[
            pltpu.VMEM((records, length), f32),
            pltpu.VMEM((length, length), bf16),
            pltpu.VMEM((length, length), bf16),
            pltpu.VMEM((length, records), f32),
            pltpu.VMEM((N_BIN, rows, records), f32),
            pltpu.VMEM((NX * NC, NZ, 4, LANES), i32),
            pltpu.VMEM((NZ, 8, LANES), f32),
            pltpu.VMEM((NX * NC, 8, LANES), f32),
            pltpu.VMEM((16 * rows, bins), f32),
            pltpu.VMEM((bins, GROUP * records), bf16),
            pltpu.VMEM((16 * rows, GROUP * records), bf16),
            pltpu.VMEM((4, 2 * rows, bins), f32),
            pltpu.SemaphoreType.DMA((3,)),
            pltpu.SemaphoreType.DMA((2 * NZ,)),
            pltpu.SemaphoreType.DMA((2 * NZ,)),
            pltpu.SemaphoreType.DMA((2 * NZ,)),
            pltpu.SemaphoreType.DMA((2 * NZ,)),
            pltpu.SemaphoreType.DMA((N_BIN,)),
            pltpu.SemaphoreType.DMA((N_BIN,)),
            pltpu.SemaphoreType.DMA((2,)),
            pltpu.SemaphoreType.DMA((2,)),
        ],
        compiler_params=pltpu.CompilerParams(
            collective_id=0, has_side_effects=True, vmem_limit_bytes=48 << 20
        ),
    )(traces[0], trace_cell, pattern, fold, jnp.asarray(high), jnp.asarray(low), jnp.asarray(sinc_table()))


def solution(mesh):
    return jax.shard_map(
        per_device,
        mesh=mesh,
        in_specs=(P("line", "bin", None), P("line", "bin"), P("line", "bin"), P("line", "bin")),
        out_specs=P("bin", "line", None),
        check_vma=False,
    )
```

time: 146 us -> 64 us (0.44); the launches traced: 144 us -> 63.7 us
  waiting for transfers between devices: 59.3 us -> 0 us
  Pallas kernels: 0 us -> 55.9 us
  starting transfers between devices: 23.9 us -> 0 us
  blocking collectives: 18.6 us -> 0 us
  other arithmetic: 15.3 us -> 0 us
  local copies, waits for them, and re-layouts: 19.4 us -> 7.83 us
  matrix products: 7.19 us -> 0 us
    pallas_call x0 -> x1, Pallas kernels: none -> 55.9 us  [per_device(): pl.pallas_call(kernel, out_shape=jax.ShapeDtypeStruct((rows, lines, bins)...]
    all_to_all x2 -> x0, waiting for transfers between devices: 55.1 us -> none  [the longest x1 48.8 us: per_device(): lax.all_to_all(outgoing, 'bin', split_axis=0, concat_axis=0, tiled=True)]
    all_to_all x1 -> x0, blocking collectives: 18.6 us -> none  [per_device(): lax.all_to_all(spectrum, 'bin', split_axis=0, concat_axis=2, tiled=True)]
    all_to_all x2 -> x0, starting transfers between devices: 17.8 us -> none  [the longest x1 13 us: per_device(): lax.all_to_all(labels, 'bin', split_axis=0, concat_axis=0, tiled=True)]
    all_to_all x7 -> x0, local copies, waits for them, and re-layouts: 8.4 us -> none  [the longest x4 7.09 us: per_device(): lax.all_to_all(spectrum, 'bin', split_axis=0, concat_axis=2, tiled=True)]
    neg x1 -> x0, other arithmetic: 8.24 us -> none  [dft_table(): return jnp.concatenate([jnp.cos(phase), -jnp.sin(phase)], axis=1) * scale]
    dot_general x3 -> x0, matrix products: 7.19 us -> none  [the longest x1 4.11 us: per_device(): jnp.dot(mixing, arrived, precision=lax.Precision.HIGHEST)]
    ppermute x2 -> x0, starting transfers between devices: 6.13 us -> none  [the longest x1 4.85 us: extended(): lax.ppermute(lax.slice_in_dim(block, block.shape[dim] - width, None, axis...]
  transfers between devices with their start and end apart: 4 -> 0, of which waited for: 4 -> 0; matrix products, arithmetic and copies ran while one was open for 10% -> 0% of each run, Pallas kernels for 0% -> 0%
where the time goes in v1:
time: 64 us; the launch traced here: 63.7 us
  Pallas kernels  55.9 us (87%)
  local copies, waits for them, and re-layouts  7.83 us (12%)
    pallas_call x1, Pallas kernels, per_device(): pl.pallas_call(kernel, out_shape=jax.ShapeDtypeStruct((rows, lines, bins)...  55.9 us
    unnamed x15, local copies, waits for them, and re-layouts  7.83 us

profile of v1, /device:TPU:1, one launch (start us, length us, event | category | flops | bytes accessed | tf_op | source)
XLA Modules:
  0.0 63.7 jit_solution(10231327721369211669)
XLA Ops:
  0.0 0.0 copy-start
  0.0 1.6 %copy-done = bf16[1024,1024]{1,0:T(8,128)(2,1)S(1)} copy-done((bf16[1024,1024]{1,0:T(8,128)(2,1)S(1)}, bf16[1024,1024]{1,0:T(8,128)(2,1)}, u32[]{:S(2)}) %copy-start) | copy-done | bytes 2097176
  1.6 0.0 copy-start.1
  1.6 1.6 %copy-done.1 = bf16[1024,1024]{1,0:T(8,128)(2,1)S(1)} copy-done((bf16[1024,1024]{1,0:T(8,128)(2,1)S(1)}, bf16[1024,1024]{1,0:T(8,128)(2,1)}, u32[]{:S(2)}) %copy-start.1) | copy-done | bytes 2097176
  3.2 0.0 copy-start.2
  3.2 1.2 %copy-done.2 = f32[1,256,1024]{2,1,0:T(8,128)S(1)} copy-done((f32[1,256,1024]{2,1,0:T(8,128)S(1)}, f32[1,256,1024]{2,1,0:T(8,128)}, u32[]{:S(2)}) %copy-start.2) | copy-done | bytes 1048600
  4.4 0.0 copy-start.3
  4.4 0.7 %copy-done.3 = f32[8,128]{1,0:T(8,128)S(1)} copy-done((f32[8,128]{1,0:T(8,128)S(1)}, f32[8,128]{1,0:T(8,128)}, u32[]{:S(2)}) %copy-start.3) | copy-done | bytes 4120
  5.1 0.0 copy-start.4
  5.1 0.7 %copy-done.4 = s32[4,16]{1,0:T(4,128)S(1)} copy-done((s32[4,16]{1,0:T(4,128)S(1)}, s32[4,16]{1,0:T(4,128)}, u32[]{:S(2)}) %copy-start.4) | copy-done | bytes 280
  5.8 0.0 copy-start.5
  5.8 0.7 %copy-done.5 = s32[1,256]{1,0:T(1,128)S(1)} copy-done((s32[1,256]{1,0:T(1,128)S(1)}, s32[1,256]{1,0:T(1,128)}, u32[]{:S(2)}) %copy-start.5) | copy-done | bytes 1048
  6.5 0.0 copy-start.6
  6.5 0.7 %copy-done.6 = s32[1,256]{1,0:T(1,128)S(1)} copy-done((s32[1,256]{1,0:T(1,128)S(1)}, s32[1,256]{1,0:T(1,128)}, u32[]{:S(2)}) %copy-start.6) | copy-done | bytes 1048
  7.1 55.9 %shard_map.73 = f32[16,4,1024]{2,1,0:T(4,128)S(1)} custom-call(f32[256,1024]{1,0:T(8,128)S(1)} %bitcast.1, s32[1,256]{1,0:T(1,128)S(1)} %copy-done.5, s32[1,256]{1,0:T(1,128)S(1)} %copy-done.6, s32[4,16]{1,0:T(4,128)S(1)} %copy-done.4, bf16[1024,1024]{1,0:T(8,128)(2,1)S(1)} %copy-done.1, bf16[1024,1024]{1,0:T(8,128)(2,1)S(1)} %copy-done, f32[8,128]{1,0:T(8,128)S(1)} %copy-done.3), custom_call_target="tpu_custom_call" | custom-call | tf_op jit(solution)/shard_map/pallas_call | solution.py:265
  63.0 0.7 %copy.9 = f32[16,4,1024]{2,1,0:T(4,128)} copy(f32[16,4,1024]{2,1,0:T(4,128)S(1)} %shard_map.73) | data formatting | bytes 524288
Async XLA Ops:
  0.0 1.6 %copy-start = (bf16[1024,1024]{1,0:T(8,128)(2,1)S(1)}, bf16[1024,1024]{1,0:T(8,128)(2,1)}, u32[]{:S(2)}) copy-start(bf16[1024,1024]{1,0:T(8,128)(2,1)} %constant.7.clone.low_hbm) | copy-start | bytes 6291460
  1.6 1.6 %copy-start.1 = (bf16[1024,1024]{1,0:T(8,128)(2,1)S(1)}, bf16[1024,1024]{1,0:T(8,128)(2,1)}, u32[]{:S(2)}) copy-start(bf16[1024,1024]{1,0:T(8,128)(2,1)} %constant.6.clone.high_hbm) | copy-start | bytes 6291460
  3.2 1.2 %copy-start.2 = (f32[1,256,1024]{2,1,0:T(8,128)S(1)}, f32[1,256,1024]{2,1,0:T(8,128)}, u32[]{:S(2)}) copy-start(f32[1,256,1024]{2,1,0:T(8,128)} %param.7) | copy-start | bytes 3145732
  4.4 0.7 %copy-start.3 = (f32[8,128]{1,0:T(8,128)S(1)}, f32[8,128]{1,0:T(8,128)}, u32[]{:S(2)}) copy-start(f32[8,128]{1,0:T(8,128)} %constant.8.clone.sinc_ref) | copy-start | bytes 12292
  5.1 0.7 %copy-start.4 = (s32[4,16]{1,0:T(4,128)S(1)}, s32[4,16]{1,0:T(4,128)}, u32[]{:S(2)}) copy-start(s32[4,16]{1,0:T(4,128)} %fold_ref.1) | copy-start | bytes 772
  5.8 0.7 %copy-start.5 = (s32[1,256]{1,0:T(1,128)S(1)}, s32[1,256]{1,0:T(1,128)}, u32[]{:S(2)}) copy-start(s32[1,256]{1,0:T(1,128)} %cell_ref.1) | copy-start | bytes 3076
  6.5 0.7 %copy-start.6 = (s32[1,256]{1,0:T(1,128)S(1)}, s32[1,256]{1,0:T(1,128)}, u32[]{:S(2)}) copy-start(s32[1,256]{1,0:T(1,128)} %pattern_ref.1) | copy-start | bytes 3076

commit v2 on v1

v2 whole, which is shorter than its diff:
```python
import functools
import math

import jax
import jax.numpy as jnp
import numpy as np
from jax import lax
from jax.experimental import pallas as pl
from jax.experimental.pallas import tpu as pltpu
from jax.sharding import PartitionSpec as P

RADIUS = 2
PATTERNS = 16
NX, NZ, NC, NY = 4, 8, 2, 4
N_BIN = NX * NZ * NC
LANES = 128
GROUP = 4
NT_DOT = (((1,), (1,)), ((), ()))
MESH = pl.DeviceIdType.MESH


def sinc_table():
    shifts = np.arange(-RADIUS, RADIUS + 1)
    offsets = (np.arange(PATTERNS) + 0.5) / PATTERNS - 0.5
    spread = shifts[:, None] - offsets[None, :]
    table = np.zeros((8, LANES), np.float32)
    table[: 2 * RADIUS + 1, :PATTERNS] = (
        np.sinc(spread) * np.cos(np.pi * spread / (2 * RADIUS + 2)) ** 2
    )
    return table


def dft_table(length):
    times = np.arange(length // 2)
    freqs = np.arange(length // 2)
    phase = 2.0 * np.pi * (freqs[:, None] * times[None, :] % length) / length
    full = np.concatenate([np.cos(phase), -np.sin(phase)], axis=0) / math.sqrt(length)
    full = full.reshape(NX, -1, 2, length // 2).transpose(0, 2, 1, 3)
    high = full.astype(jnp.bfloat16)
    low = (full - high.astype(np.float64)).astype(jnp.bfloat16)
    return np.concatenate([high, low], axis=2)


def split(values):
    high = values.astype(jnp.bfloat16)
    return high, (values - high.astype(jnp.float32)).astype(jnp.bfloat16)


def dot_nt(a, b):
    return lax.dot_general(a, b, NT_DOT, preferred_element_type=jnp.float32)


def place():
    b = lax.axis_index("bin")
    return b // (NZ * NC), b // NC % NZ, b % NC, lax.axis_index("line")


def device(x, z, c):
    return (x * NZ + z) * NC + c


def kernel(
    traces_hbm, cell_hbm, pattern_hbm, fold_hbm, table_hbm, sinc_hbm,
    out_ref,
    traces, cells, patterns, own_fold, table, sinc, spec, recv, meta, folds, fold_sum, acc, onehot, mixed, halo,
    load_sem, entered, meta_ssem, meta_rsem, fold_ssem, fold_rsem, send_sem, recv_sem, halo_ssem, halo_rsem,
):
    bins = acc.shape[1]
    x, z, c, y = place()
    me = device(x, z, c)
    above, below = (y + 1) % NY, (y + NY - 1) % NY
    columns = NX * NC

    def along_z(k):
        return device(x, (z + k) % NZ, c), y

    def across(k):
        return device((x + k // NC) % NX, z, (c + k) % NC), y

    barrier = pltpu.get_barrier_semaphore()
    neighbours = [along_z(k) for k in range(1, NZ)] + [across(k) for k in range(1, columns)]
    neighbours += [(me, above), (me, below)]
    for other in neighbours:
        pl.semaphore_signal(barrier, inc=1, device_id=other, device_id_type=MESH)

    pairs = [(cell_hbm, cells), (pattern_hbm, patterns), (traces_hbm, traces)]
    pairs += [(table_hbm.at[(x + i) % NX], table.at[i]) for i in range(NX)]
    pairs += [(fold_hbm, own_fold), (sinc_hbm, sinc)]
    loads = [
        pltpu.make_async_copy(source, target, load_sem.at[i])
        for i, (source, target) in enumerate(pairs)
    ]
    for load in loads:
        load.start()

    loads[0].wait()
    loads[1].wait()
    for i in range(2):
        meta[0, 0, pl.ds(i, 1), :] = cells[:, pl.ds(i * LANES, LANES)]
        meta[0, 0, pl.ds(2 + i, 1), :] = patterns[:, pl.ds(i * LANES, LANES)]

    pl.semaphore_wait(barrier, len(neighbours))
    for k in range(1, columns):
        pl.semaphore_signal(entered, inc=1, device_id=across(k), device_id_type=MESH)
    meta_along = [
        pltpu.make_async_remote_copy(
            meta.at[0, 0], meta.at[0, k], meta_ssem.at[k], meta_rsem.at[k],
            device_id=along_z(k), device_id_type=MESH)
        for k in range(1, NZ)
    ]
    for copy in meta_along:
        copy.start()

    loads[2].wait()
    middle = traces.shape[1] // 2
    early, late = traces[:, :middle], traces[:, middle:]
    parts = [split(early + late), split(early - late)]

    def transform(i):
        loads[3 + i].wait()
        for parity, (t_high, t_low) in enumerate(parts):
            both = dot_nt(table[i, parity], t_high)
            rows = both.shape[0] // 2
            value = both[:rows] + both[rows:] + dot_nt(table[i, parity, :rows], t_low)
            at = pl.ds((x + i) % NX * (NZ * NC), NZ * NC)
            spec[at, parity] = value.reshape(NZ * NC, rows // (NZ * NC), -1)

    def sent(k):
        a, d = k // NZ, k % NZ
        target = device((x + a // NC) % NX, (z + d) % NZ, (c + a) % NC)
        return pltpu.make_async_remote_copy(
            spec.at[target], recv.at[k], send_sem.at[k], recv_sem.at[k],
            device_id=(target, y), device_id_type=MESH)

    def start_one(k, carry):
        sent(k).start()
        return carry

    transform(0)
    lax.fori_loop(1, NZ, start_one, 0)
    pl.semaphore_wait(entered, columns - 1)
    lax.fori_loop(NZ, NZ * NC, start_one, 0)
    for copy in meta_along:
        copy.wait_recv()
    meta_across = [
        pltpu.make_async_remote_copy(
            meta.at[0], meta.at[k], meta_ssem.at[NZ + k], meta_rsem.at[NZ + k],
            device_id=across(k), device_id_type=MESH)
        for k in range(1, columns)
    ]
    for copy in meta_across:
        copy.start()
    for i in range(1, NX):
        transform(i)
        lax.fori_loop(NZ * NC * i, NZ * NC * (i + 1), start_one, 0)
    recv[0] = spec[me]

    loads[-1].wait()
    loads[-2].wait()
    lanes = own_fold.shape[1]
    spread_row = lax.broadcasted_iota(jnp.int32, (lanes, LANES), 0)
    spread_lane = lax.broadcasted_iota(jnp.int32, (lanes, LANES), 1)
    spread = (spread_lane == (z % 4) * (NC * lanes) + c * lanes + spread_row).astype(jnp.float32)
    fold_row = jnp.dot(
        own_fold[...].astype(jnp.float32), spread, preferred_element_type=jnp.float32
    )
    fold_both = jnp.concatenate([fold_row, fold_row], axis=0)
    half = lax.broadcasted_iota(jnp.int32, fold_both.shape, 0) // 4
    folds[0] = jnp.where(half == z // 4, fold_both, 0.0)
    fold_along = [
        pltpu.make_async_remote_copy(
            folds.at[0], folds.at[k], fold_ssem.at[k], fold_rsem.at[k],
            device_id=along_z(k), device_id_type=MESH)
        for k in range(1, NZ)
    ]
    for copy in fold_along:
        copy.start()
    acc[...] = jnp.zeros_like(acc)
    for copy in meta_across:
        copy.wait_recv()
    for copy in fold_along:
        copy.wait_recv()
    fold_sum[0] = jnp.sum(folds[...], axis=0)
    fold_across = [
        pltpu.make_async_remote_copy(
            fold_sum.at[0], fold_sum.at[k], fold_ssem.at[NZ + k], fold_rsem.at[NZ + k],
            device_id=across(k), device_id_type=MESH)
        for k in range(1, columns)
    ]
    for copy in fold_across:
        copy.start()

    slice_rows = recv.shape[1] * recv.shape[2]
    records = recv.shape[3]
    full = 8 * slice_rows

    def stack(i, carry):
        weights = []
        for j in range(GROUP):
            k = i * GROUP + j
            tags = meta[k // NZ, k % NZ]
            cell = jnp.concatenate([tags[0:1], tags[1:2]], axis=1)
            pattern = jnp.broadcast_to(
                jnp.concatenate([tags[2:3], tags[3:4]], axis=1), (8, records)
            )
            taps = jnp.zeros((8, records), jnp.float32)
            for q in range(PATTERNS):
                taps = jnp.where(pattern == q, sinc[:, q : q + 1], taps)
            line = jnp.broadcast_to(cell // bins, (8, records))
            shifted = taps
            for s in range(1, 4):
                shifted = jnp.where(line == s, pltpu.roll(taps, s, 0), shifted)
            weights.append(shifted)
            where = cell % bins
            for g in range(0, bins, 256):
                row = lax.broadcasted_iota(jnp.int32, (256, records), 0) + g
                onehot[pl.ds(g, 256), pl.ds(j * records, records)] = (
                    (row == jnp.broadcast_to(where, (256, records)))
                    .astype(jnp.float32)
                    .astype(jnp.bfloat16)
                )
        for j in range(GROUP):
            k = i * GROUP + j

            @pl.when(k > 0)
            def _():
                sent(k).wait_recv()

            block = recv[k].reshape(slice_rows, records)
            terms = (weights[j][:, None, :] * block[None, :, :]).reshape(full, records)
            t_high, t_low = split(terms)
            mixed[pl.ds(0, full), pl.ds(j * records, records)] = t_high
            mixed[pl.ds(full, full), pl.ds(j * records, records)] = t_low
        for g in range(0, bins, 256):
            acc[:, pl.ds(g, 256)] += dot_nt(mixed[...], onehot[pl.ds(g, 256), :])
        return carry

    lax.fori_loop(0, N_BIN // GROUP, stack, 0)

    edge = 2 * slice_rows
    halo[0] = acc[pl.ds(0, edge), :] + acc[pl.ds(full, edge), :]
    halo[1] = acc[pl.ds(full - edge, edge), :] + acc[pl.ds(2 * full - edge, edge), :]
    down = pltpu.make_async_remote_copy(
        halo.at[0], halo.at[2], halo_ssem.at[0], halo_rsem.at[0],
        device_id=(me, below), device_id_type=MESH)
    up = pltpu.make_async_remote_copy(
        halo.at[1], halo.at[3], halo_ssem.at[1], halo_rsem.at[1],
        device_id=(me, above), device_id_type=MESH)
    down.start()
    up.start()
    for copy in fold_across:
        copy.wait_recv()
    counts = []
    for i in range(NX):
        slot = (x + NX - i) % NX * NC
        counts.append(fold_sum[slot] + fold_sum[slot + 1])
    inverse = 1.0 / jnp.concatenate(
        [block[4 * h : 4 * h + 4] for block in counts for h in range(2)], axis=1
    )

    def finish_one(k, carry):
        sent(k).wait_send()
        return carry

    lax.fori_loop(1, N_BIN, finish_one, 0)
    for copy in meta_along + meta_across + fold_along + fold_across:
        copy.wait_send()
    down.wait()
    up.wait()
    for line in range(4):
        value = acc[pl.ds((line + 2) * slice_rows, slice_rows), :]
        value = value + acc[pl.ds(full + (line + 2) * slice_rows, slice_rows), :]
        if line < 2:
            extra = halo[3, pl.ds(line * slice_rows, slice_rows), :]
            inside = y > 0
        else:
            extra = halo[2, pl.ds((line - 2) * slice_rows, slice_rows), :]
            inside = y < NY - 1
        value = (value + jnp.where(inside, extra, 0.0)) * inverse[line : line + 1, :]
        for parity in range(2):
            out_ref[:, parity, line, :] = value[parity * 8 : parity * 8 + 8]


def per_device(traces, trace_cell, pattern, fold):
    _, records, length = traces.shape
    lines, bins_dev = fold.shape
    bins = bins_dev * N_BIN
    rows = length // N_BIN
    table = dft_table(length)
    anywhere = pl.BlockSpec(memory_space=pl.ANY)
    f32, i32, bf16 = jnp.float32, jnp.int32, jnp.bfloat16
    dma = pltpu.SemaphoreType.DMA
    out = pl.pallas_call(
        kernel,
        out_shape=jax.ShapeDtypeStruct((rows // 2, 2, lines, bins), f32),
        in_specs=[anywhere] * 6,
        out_specs=pl.BlockSpec(memory_space=pltpu.VMEM),
        scratch_shapes=[
            pltpu.VMEM((records, length), f32),
            pltpu.VMEM((1, records), i32),
            pltpu.VMEM((1, records), i32),
            pltpu.VMEM((lines, bins_dev), i32),
            pltpu.VMEM(table.shape, bf16),
            pltpu.VMEM((8, LANES), f32),
            pltpu.VMEM((N_BIN, 2, rows // 2, records), f32),
            pltpu.VMEM((N_BIN, 2, rows // 2, records), f32),
            pltpu.VMEM((NX * NC, NZ, 4, LANES), i32),
            pltpu.VMEM((NZ, 8, LANES), f32),
            pltpu.VMEM((NX * NC, 8, LANES), f32),
            pltpu.VMEM((16 * rows, bins), f32),
            pltpu.VMEM((bins, GROUP * records), bf16),
            pltpu.VMEM((16 * rows, GROUP * records), bf16),
            pltpu.VMEM((4, 2 * rows, bins), f32),
            dma((5 + NX,)),
            pltpu.SemaphoreType.REGULAR,
            dma((2 * NZ,)),
            dma((2 * NZ,)),
            dma((2 * NZ,)),
            dma((2 * NZ,)),
            dma((N_BIN,)),
            dma((N_BIN,)),
            dma((2,)),
            dma((2,)),
        ],
        compiler_params=pltpu.CompilerParams(
            collective_id=0, has_side_effects=True, vmem_limit_bytes=63 << 20
        ),
    )(traces[0], trace_cell, pattern, fold, jnp.asarray(table), jnp.asarray(sinc_table()))
    return out.reshape(rows, lines, bins)


def solution(mesh):
    return jax.shard_map(
        per_device,
        mesh=mesh,
        in_specs=(P("line", "bin", None), P("line", "bin"), P("line", "bin"), P("line", "bin")),
        out_specs=P("bin", "line", None),
        check_vma=False,
    )
```

time: 64 us -> 69.4 us (1.084)
  Pallas kernels: 55.9 us -> 67 us
  local copies, waits for them, and re-layouts: 7.83 us -> 1.67 us
    pallas_call x1, Pallas kernels: 55.9 us -> 67 us  [per_device(): pl.pallas_call(kernel, out_shape=jax.ShapeDtypeStruct((rows // 2, 2, line...]
    unnamed x15 -> x1, local copies, waits for them, and re-layouts: 7.83 us -> 1.67 us
where the time goes in v2:
time: 69.4 us; the launch traced here: 68.7 us
  Pallas kernels  67 us (97%)
  local copies, waits for them, and re-layouts  1.67 us (2%)
    pallas_call x1, Pallas kernels, per_device(): pl.pallas_call(kernel, out_shape=jax.ShapeDtypeStruct((rows // 2, 2, line...  67 us
    unnamed x1, local copies, waits for them, and re-layouts  1.67 us

profile of v2, /device:TPU:1, one launch (start us, length us, event | category | flops | bytes accessed | tf_op | source)
XLA Modules:
  0.0 68.7 jit_solution(13667099567244881455)
XLA Ops:
  0.0 67.0 %shard_map.64 = f32[8,2,4,1024]{3,2,1,0:T(4,128)} custom-call(f32[256,1024]{1,0:T(8,128)} %bitcast.2, s32[1,256]{1,0:T(1,128)} %cell_hbm.1, s32[1,256]{1,0:T(1,128)} %pattern_hbm.1, s32[4,16]{1,0:T(4,128)} %fold_hbm.1, bf16[4,2,256,512]{3,2,1,0:T(8,128)(2,1)} %constant.4.clone.table_hbm, f32[8,128]{1,0:T(8,128)} %constant.5.clone.sinc_hbm), custom_call_target="tpu_custom_call" | custom-call | tf_op jit(solution)/shard_map/pallas_call | solution.py:293
  67.1 1.7 %copy.8 = f32[16,4,1024]{2,1,0:T(4,128)} copy(f32[16,4,1024]{2,1,0:T(4,128)} %bitcast.3) | data formatting | bytes 524288

commit v3 on v2

v3 whole, which is shorter than its diff:
```python
import functools
import math

import jax
import jax.numpy as jnp
import numpy as np
from jax import lax
from jax.experimental import pallas as pl
from jax.experimental.pallas import tpu as pltpu
from jax.sharding import PartitionSpec as P

RADIUS = 2
PATTERNS = 16
NX, NZ, NC, NY = 4, 8, 2, 4
N_BIN = NX * NZ * NC
LANES = 128
GROUP = 8
LAST = 4
NT_DOT = (((1,), (1,)), ((), ()))
MESH = pl.DeviceIdType.MESH


def sinc_table():
    shifts = np.arange(-RADIUS, RADIUS + 1)
    offsets = (np.arange(PATTERNS) + 0.5) / PATTERNS - 0.5
    spread = shifts[:, None] - offsets[None, :]
    table = np.zeros((8, LANES), np.float32)
    table[: 2 * RADIUS + 1, :PATTERNS] = (
        np.sinc(spread) * np.cos(np.pi * spread / (2 * RADIUS + 2)) ** 2
    )
    return table


def dft_table(length):
    times = np.arange(length // 2)
    freqs = np.arange(length // 2)
    phase = 2.0 * np.pi * (freqs[:, None] * times[None, :] % length) / length
    full = np.concatenate([np.cos(phase), -np.sin(phase)], axis=0) / math.sqrt(length)
    full = full.reshape(NX, -1, 2, length // 2).transpose(0, 2, 1, 3)
    high = full.astype(jnp.bfloat16)
    low = (full - high.astype(np.float64)).astype(jnp.bfloat16)
    return np.concatenate([high, low], axis=2)


def split(values):
    high = values.astype(jnp.bfloat16)
    return high, (values - high.astype(jnp.float32)).astype(jnp.bfloat16)


def dot_nt(a, b):
    return lax.dot_general(a, b, NT_DOT, preferred_element_type=jnp.float32)


def place():
    b = lax.axis_index("bin")
    return b // (NZ * NC), b // NC % NZ, b % NC, lax.axis_index("line")


def device(x, z, c):
    return (x * NZ + z) * NC + c


X_ORDER = (0, 2, 1, 3)
OWN = NZ * NC - NC


def offsets(k):
    i, d, e = k // (NZ * NC), k // NC % NZ, k % NC
    along_x = jnp.where(i == 1, X_ORDER[1], jnp.where(i == 2, X_ORDER[2], i))
    along_z = NZ // 2 + jnp.where(d % 2 == 1, -((d + 1) // 2), d // 2)
    return along_x, along_z, e


def unit_of(k):
    late = k - (N_BIN - 2 * LAST)
    return jnp.where(late < 0, k // GROUP, (N_BIN - 2 * LAST) // GROUP + late // LAST)


def wait_for(ref, sem):
    pltpu.make_async_copy(ref, ref, sem).wait()


def kernel(
    traces_hbm, cell_hbm, pattern_hbm, fold_hbm, table_hbm, sinc_hbm,
    out_ref,
    traces, cells, patterns, own_fold, table, sinc, spec, recv, meta, folds, fold_sum, acc, onehot, mixed, halo,
    load_sem, entered, meta_sem, fold_sem, send_sem, recv_sem, halo_sem,
):
    bins = acc.shape[1]
    x, z, c, y = place()
    me = device(x, z, c)
    above, below = (y + 1) % NY, (y + NY - 1) % NY
    columns = NX * NC

    def along_z(k):
        return device(x, (z + k) % NZ, c), y

    def across(k):
        return device((x + k // NC) % NX, z, (c + k) % NC), y

    def copies(ref, slots, peer, sem):
        for k in range(1, slots):
            pltpu.make_async_remote_copy(
                ref.at[0], ref.at[k], sem.at[0], sem.at[1],
                device_id=peer(k), device_id_type=MESH).start()

    barrier = pltpu.get_barrier_semaphore()
    neighbours = [along_z(k) for k in range(1, NZ)] + [across(k) for k in range(1, columns)]
    neighbours += [(me, above), (me, below)]
    for other in neighbours:
        pl.semaphore_signal(barrier, inc=1, device_id=other, device_id_type=MESH)

    pairs = [(cell_hbm, cells), (pattern_hbm, patterns), (fold_hbm, own_fold), (traces_hbm, traces)]
    pairs += [(table_hbm.at[(x + i) % NX], table.at[n]) for n, i in enumerate(X_ORDER)]
    pairs += [(sinc_hbm, sinc)]
    loads = [
        pltpu.make_async_copy(source, target, load_sem.at[i])
        for i, (source, target) in enumerate(pairs)
    ]
    for load in loads:
        load.start()

    pl.semaphore_wait(barrier, len(neighbours))
    for k in range(1, columns):
        pl.semaphore_signal(entered, inc=1, device_id=across(k), device_id_type=MESH)

    loads[0].wait()
    loads[1].wait()
    for i in range(2):
        meta[0, 0, pl.ds(i, 1), :] = cells[:, pl.ds(i * LANES, LANES)]
        meta[0, 0, pl.ds(2 + i, 1), :] = patterns[:, pl.ds(i * LANES, LANES)]
    copies(meta.at[0], NZ, along_z, meta_sem.at[0])
    loads[2].wait()
    lanes = own_fold.shape[1]
    spread_row = lax.broadcasted_iota(jnp.int32, (lanes, LANES), 0)
    spread_lane = lax.broadcasted_iota(jnp.int32, (lanes, LANES), 1)
    spread = (spread_lane == (z % 4) * (NC * lanes) + c * lanes + spread_row).astype(jnp.float32)
    fold_row = jnp.dot(
        own_fold[...].astype(jnp.float32), spread, preferred_element_type=jnp.float32
    )
    fold_both = jnp.concatenate([fold_row, fold_row], axis=0)
    half = lax.broadcasted_iota(jnp.int32, fold_both.shape, 0) // 4
    folds[0] = jnp.where(half == z // 4, fold_both, 0.0)
    copies(folds, NZ, along_z, fold_sem.at[0])

    loads[3].wait()
    middle = traces.shape[1] // 2
    early, late = traces[:, :middle], traces[:, middle:]
    parts = [split(early + late), split(early - late)]

    def transform(i):
        loads[4 + i].wait()
        for parity, (t_high, t_low) in enumerate(parts):
            both = dot_nt(table[i, parity], t_high)
            rows = both.shape[0] // 2
            value = both[:rows] + both[rows:] + dot_nt(table[i, parity, :rows], t_low)
            at = pl.ds((x + X_ORDER[i]) % NX * (NZ * NC), NZ * NC)
            spec[at, parity] = value.reshape(NZ * NC, rows // (NZ * NC), -1)

    def start(k):
        i, d, e = offsets(k)
        target = device((x + i) % NX, (z + d) % NZ, (c + e) % NC)
        pltpu.make_async_remote_copy(
            spec.at[target], recv.at[k], send_sem.at[0], recv_sem.at[unit_of(k)],
            device_id=(target, y), device_id_type=MESH).start()

    def start_one(k, carry):
        start(k)
        return carry

    transform(0)
    for d in range(NZ - 1):
        start(d * NC)
    pltpu.make_async_copy(spec.at[me], recv.at[OWN], recv_sem.at[unit_of(OWN)]).start()
    pl.semaphore_wait(entered, columns - 1)
    for d in range(NZ):
        start(d * NC + 1)
    wait_for(meta.at[0, pl.ds(1, NZ - 1)], meta_sem.at[0, 1])
    copies(meta, columns, across, meta_sem.at[1])
    wait_for(folds.at[pl.ds(1, NZ - 1)], fold_sem.at[0, 1])
    fold_sum[0] = jnp.sum(folds[...], axis=0)
    copies(fold_sum, columns, across, fold_sem.at[1])
    for i in range(1, NX):
        transform(i)
        lax.fori_loop(i * NZ * NC, (i + 1) * NZ * NC, start_one, 0)

    loads[-1].wait()
    acc[...] = jnp.zeros_like(acc)
    wait_for(meta.at[pl.ds(1, columns - 1)], meta_sem.at[1, 1])

    slice_rows = recv.shape[1] * recv.shape[2]
    records = recv.shape[3]
    full = 8 * slice_rows

    def tags_of(k):
        i, d, e = offsets(k)
        tags = meta[i * NC + e, d]
        return (
            jnp.concatenate([tags[0:1], tags[1:2]], axis=1),
            jnp.concatenate([tags[2:3], tags[3:4]], axis=1),
        )

    def weigh(cell, pattern):
        pattern = jnp.broadcast_to(pattern, (8, records))
        taps = jnp.zeros((8, records), jnp.float32)
        for q in range(PATTERNS):
            taps = jnp.where(pattern == q, sinc[:, q : q + 1], taps)
        line = jnp.broadcast_to(cell // bins, (8, records))
        weights = taps
        for s in range(1, 4):
            weights = jnp.where(line == s, pltpu.roll(taps, s, 0), weights)
        return jnp.concatenate([weights[0:2], weights[6:8], weights[2:6]], axis=0)

    def mark(j, cell):
        where = cell % bins
        for g in range(0, bins, 256):
            row = lax.broadcasted_iota(jnp.int32, (256, records), 0) + g
            onehot[pl.ds(g, 256), pl.ds(j * records, records)] = (
                (row == jnp.broadcast_to(where, (256, records)))
                .astype(jnp.float32)
                .astype(jnp.bfloat16)
            )

    def mix(k, j, weights):
        block = recv[k].reshape(slice_rows, records)
        terms = (weights[:, None, :] * block[None, :, :]).reshape(full, records)
        t_high, t_low = split(terms)
        at = pl.ds(j * records, records)
        edge = full // 2
        mixed[pl.ds(0, edge), at] = t_high[:edge]
        mixed[pl.ds(edge, edge), at] = t_low[:edge]
        mixed[pl.ds(2 * edge, edge), at] = t_high[edge:]
        mixed[pl.ds(3 * edge, edge), at] = t_low[edge:]

    def add(rows, count):
        depth = pl.ds(0, count * records)
        for g in range(0, bins, 256):
            acc[rows, pl.ds(g, 256)] += dot_nt(mixed[rows, depth], onehot[pl.ds(g, 256), depth])

    def stack(i, carry):
        wait_for(recv.at[pl.ds(i * GROUP, GROUP)], recv_sem.at[i])
        for j in range(GROUP):
            k = i * GROUP + j
            cell, pattern = tags_of(k)
            mix(k, j, weigh(cell, pattern))
            mark(j, cell)
        add(pl.ds(0, 2 * full), GROUP)
        return carry

    whole = (N_BIN - 2 * LAST) // GROUP
    lax.fori_loop(0, whole, stack, 0)

    def prepare(at):
        weights = []
        for j in range(LAST):
            cell, pattern = tags_of(at + j)
            weights.append(weigh(cell, pattern))
            mark(j, cell)
        return weights

    weights = prepare(N_BIN - 2 * LAST)
    wait_for(recv.at[pl.ds(N_BIN - 2 * LAST, LAST)], recv_sem.at[whole])
    for j in range(LAST):
        mix(N_BIN - 2 * LAST + j, j, weights[j])
    add(pl.ds(0, 2 * full), LAST)
    weights = prepare(N_BIN - LAST)
    wait_for(fold_sum.at[pl.ds(1, columns - 1)], fold_sem.at[1, 1])
    counts = []
    for i in range(NX):
        slot = (x + NX - i) % NX * NC
        counts.append(fold_sum[slot] + fold_sum[slot + 1])
    inverse = 1.0 / jnp.concatenate(
        [block[4 * h : 4 * h + 4] for block in counts for h in range(2)], axis=1
    )
    wait_for(recv.at[pl.ds(N_BIN - LAST, LAST)], recv_sem.at[whole + 1])
    for j in range(LAST):
        mix(N_BIN - LAST + j, j, weights[j])
    add(pl.ds(0, full), LAST)
    edge = 2 * slice_rows
    for i in range(2):
        halo[i] = acc[pl.ds(i * edge, edge), :] + acc[pl.ds((2 + i) * edge, edge), :]
    swaps = [
        pltpu.make_async_remote_copy(
            halo.at[i], halo.at[2 + i], halo_sem.at[0, i], halo_sem.at[1, i],
            device_id=(me, other), device_id_type=MESH)
        for i, other in enumerate((below, above))
    ]
    for swap in swaps:
        swap.start()
    add(pl.ds(full, full), LAST)
    wait_for(meta.at[0, pl.ds(1, NZ - 1)], meta_sem.at[0, 0])
    wait_for(meta.at[pl.ds(1, columns - 1)], meta_sem.at[1, 0])
    wait_for(folds.at[pl.ds(1, NZ - 1)], fold_sem.at[0, 0])
    wait_for(fold_sum.at[pl.ds(1, columns - 1)], fold_sem.at[1, 0])
    wait_for(recv.at[pl.ds(1, N_BIN - 1)], send_sem.at[0])
    for swap in swaps:
        swap.wait()
    for line in range(4):
        at = full + line * slice_rows
        value = acc[pl.ds(at, slice_rows), :] + acc[pl.ds(at + full // 2, slice_rows), :]
        if line < 2:
            extra = halo[3, pl.ds(line * slice_rows, slice_rows), :]
            inside = y > 0
        else:
            extra = halo[2, pl.ds((line - 2) * slice_rows, slice_rows), :]
            inside = y < NY - 1
        value = (value + jnp.where(inside, extra, 0.0)) * inverse[line : line + 1, :]
        for parity in range(2):
            out_ref[:, parity, line, :] = value[parity * 8 : parity * 8 + 8]


def per_device(traces, trace_cell, pattern, fold):
    _, records, length = traces.shape
    lines, bins_dev = fold.shape
    bins = bins_dev * N_BIN
    rows = length // N_BIN
    table = dft_table(length)
    anywhere = pl.BlockSpec(memory_space=pl.ANY)
    f32, i32, bf16 = jnp.float32, jnp.int32, jnp.bfloat16
    dma = pltpu.SemaphoreType.DMA
    out = pl.pallas_call(
        kernel,
        out_shape=jax.ShapeDtypeStruct((rows // 2, 2, lines, bins), f32),
        in_specs=[anywhere] * 6,
        out_specs=pl.BlockSpec(memory_space=pltpu.VMEM),
        scratch_shapes=[
            pltpu.VMEM((records, length), f32),
            pltpu.VMEM((1, records), i32),
            pltpu.VMEM((1, records), i32),
            pltpu.VMEM((lines, bins_dev), i32),
            pltpu.VMEM(table.shape, bf16),
            pltpu.VMEM((8, LANES), f32),
            pltpu.VMEM((N_BIN, 2, rows // 2, records), f32),
            pltpu.VMEM((N_BIN, 2, rows // 2, records), f32),
            pltpu.VMEM((NX * NC, NZ, 4, LANES), i32),
            pltpu.VMEM((NZ, 8, LANES), f32),
            pltpu.VMEM((NX * NC, 8, LANES), f32),
            pltpu.VMEM((16 * rows, bins), f32),
            pltpu.VMEM((bins, GROUP * records), bf16),
            pltpu.VMEM((16 * rows, GROUP * records), bf16),
            pltpu.VMEM((4, 2 * rows, bins), f32),
            dma((5 + NX,)),
            pltpu.SemaphoreType.REGULAR,
            dma((2, 2)),
            dma((2, 2)),
            dma((1,)),
            dma((N_BIN // GROUP + 1,)),
            dma((2, 2)),
        ],
        compiler_params=pltpu.CompilerParams(
            collective_id=0, has_side_effects=True, vmem_limit_bytes=63 << 20
        ),
    )(traces[0], trace_cell, pattern, fold, jnp.asarray(table), jnp.asarray(sinc_table()))
    return out.reshape(rows, lines, bins)


def solution(mesh):
    return jax.shard_map(
        per_device,
        mesh=mesh,
        in_specs=(P("line", "bin", None), P("line", "bin"), P("line", "bin"), P("line", "bin")),
        out_specs=P("bin", "line", None),
        check_vma=False,
    )
```

time: 69.4 us -> 48.8 us (0.70)
  Pallas kernels: 67 us -> 47 us
    pallas_call x1, Pallas kernels: 67 us -> 47 us  [per_device(): pl.pallas_call(kernel, out_shape=jax.ShapeDtypeStruct((rows // 2, 2, line...]
where the time goes in v3:
time: 48.8 us; the launch traced here: 48.7 us
  Pallas kernels  47 us (96%)
  local copies, waits for them, and re-layouts  1.67 us (3%)
    pallas_call x1, Pallas kernels, per_device(): pl.pallas_call(kernel, out_shape=jax.ShapeDtypeStruct((rows // 2, 2, line...  47 us
    unnamed x1, local copies, waits for them, and re-layouts  1.67 us

profile of v3, /device:TPU:1, one launch (start us, length us, event | category | flops | bytes accessed | tf_op | source)
XLA Modules:
  0.0 48.7 jit_solution(15423887016976574060)
XLA Ops:
  0.0 47.0 %shard_map.64 = f32[8,2,4,1024]{3,2,1,0:T(4,128)} custom-call(f32[256,1024]{1,0:T(8,128)} %bitcast.2, s32[1,256]{1,0:T(1,128)} %cell_hbm.1, s32[1,256]{1,0:T(1,128)} %pattern_hbm.1, s32[4,16]{1,0:T(4,128)} %fold_hbm.1, bf16[4,2,256,512]{3,2,1,0:T(8,128)(2,1)} %constant.4.clone.table_hbm, f32[8,128]{1,0:T(8,128)} %constant.5.clone.sinc_hbm), custom_call_target="tpu_custom_call" | custom-call | tf_op jit(solution)/shard_map/pallas_call | solution.py:321
  47.0 1.7 %copy.8 = f32[16,4,1024]{2,1,0:T(4,128)} copy(f32[16,4,1024]{2,1,0:T(4,128)} %bitcast.3) | data formatting | bytes 524288

commit v4 on v3

--- a/solution.py
+++ b/solution.py
@@ -106,9 +106,16 @@
 
     barrier = pltpu.get_barrier_semaphore()
     neighbours = [along_z(k) for k in range(1, NZ)] + [across(k) for k in range(1, columns)]
-    neighbours += [(me, above), (me, below)]
     for other in neighbours:
         pl.semaphore_signal(barrier, inc=1, device_id=other, device_id_type=MESH)
+
+    @pl.when(y > 0)
+    def _():
+        pl.semaphore_signal(barrier, inc=1, device_id=(me, below), device_id_type=MESH)
+
+    @pl.when(y < NY - 1)
+    def _():
+        pl.semaphore_signal(barrier, inc=1, device_id=(me, above), device_id_type=MESH)
 
     pairs = [(cell_hbm, cells), (pattern_hbm, patterns), (fold_hbm, own_fold), (traces_hbm, traces)]
     pairs += [(table_hbm.at[(x + i) % NX], table.at[n]) for n, i in enumerate(X_ORDER)]
@@ -120,7 +127,8 @@
     for load in loads:
         load.start()
 
-    pl.semaphore_wait(barrier, len(neighbours))
+    both_sides = jnp.where((y > 0) & (y < NY - 1), 2, 1)
+    pl.semaphore_wait(barrier, len(neighbours) + both_sides)
     for k in range(1, columns):
         pl.semaphore_signal(entered, inc=1, device_id=across(k), device_id_type=MESH)
 
@@ -232,9 +240,9 @@
         mixed[pl.ds(2 * edge, edge), at] = t_high[edge:]
         mixed[pl.ds(3 * edge, edge), at] = t_low[edge:]
 
-    def add(rows, count):
+    def add(rows, count, first=0, end=bins):
         depth = pl.ds(0, count * records)
-        for g in range(0, bins, 256):
+        for g in range(first, end, 256):
             acc[rows, pl.ds(g, 256)] += dot_nt(mixed[rows, depth], onehot[pl.ds(g, 256), depth])
 
     def stack(i, carry):
@@ -275,38 +283,55 @@
     wait_for(recv.at[pl.ds(N_BIN - LAST, LAST)], recv_sem.at[whole + 1])
     for j in range(LAST):
         mix(N_BIN - LAST + j, j, weights[j])
-    add(pl.ds(0, full), LAST)
     edge = 2 * slice_rows
-    for i in range(2):
-        halo[i] = acc[pl.ds(i * edge, edge), :] + acc[pl.ds((2 + i) * edge, edge), :]
-    swaps = [
-        pltpu.make_async_remote_copy(
-            halo.at[i], halo.at[2 + i], halo_sem.at[0, i], halo_sem.at[1, i],
-            device_id=(me, other), device_id_type=MESH)
-        for i, other in enumerate((below, above))
-    ]
-    for swap in swaps:
-        swap.start()
+    part = bins // 2
+    swaps = []
+    for p in range(2):
+        at = pl.ds(p * part, part)
+        add(pl.ds(0, full), LAST, p * part, (p + 1) * part)
+        for i in range(2):
+            halo[p, i] = acc[pl.ds(i * edge, edge), at] + acc[pl.ds((2 + i) * edge, edge), at]
+        down, up = [
+            pltpu.make_async_remote_copy(
+                halo.at[p, i], halo.at[p, 2 + i], halo_sem.at[p, i], halo_sem.at[p, 2 + i],
+                device_id=(me, other), device_id_type=MESH)
+            for i, other in enumerate((below, above))
+        ]
+        pl.when(y > 0)(down.start)
+        pl.when(y < NY - 1)(up.start)
+        swaps.append((down, up))
     add(pl.ds(full, full), LAST)
     wait_for(meta.at[0, pl.ds(1, NZ - 1)], meta_sem.at[0, 0])
     wait_for(meta.at[pl.ds(1, columns - 1)], meta_sem.at[1, 0])
     wait_for(folds.at[pl.ds(1, NZ - 1)], fold_sem.at[0, 0])
     wait_for(fold_sum.at[pl.ds(1, columns - 1)], fold_sem.at[1, 0])
     wait_for(recv.at[pl.ds(1, N_BIN - 1)], send_sem.at[0])
-    for swap in swaps:
-        swap.wait()
-    for line in range(4):
-        at = full + line * slice_rows
-        value = acc[pl.ds(at, slice_rows), :] + acc[pl.ds(at + full // 2, slice_rows), :]
-        if line < 2:
-            extra = halo[3, pl.ds(line * slice_rows, slice_rows), :]
-            inside = y > 0
-        else:
-            extra = halo[2, pl.ds((line - 2) * slice_rows, slice_rows), :]
-            inside = y < NY - 1
-        value = (value + jnp.where(inside, extra, 0.0)) * inverse[line : line + 1, :]
-        for parity in range(2):
-            out_ref[:, parity, line, :] = value[parity * 8 : parity * 8 + 8]
+    for p, (down, up) in enumerate(swaps):
+
+        @pl.when(y > 0)
+        def _():
+            down.wait_send()
+            up.wait_recv()
+
+        @pl.when(y < NY - 1)
+        def _():
+            up.wait_send()
+            down.wait_recv()
+
+        at = pl.ds(p * part, part)
+        for line in range(4):
+            rows = full + line * slice_rows
+            value = acc[pl.ds(rows, slice_rows), at] + acc[pl.ds(rows + full // 2, slice_rows), at]
+            if line < 2:
+                extra = halo[p, 3, pl.ds(line * slice_rows, slice_rows), :]
+                inside = y > 0
+            else:
+                extra = halo[p, 2, pl.ds((line - 2) * slice_rows, slice_rows), :]
+                inside = y < NY - 1
+            scale = inverse[line : line + 1, p * part : (p + 1) * part]
+            value = (value + jnp.where(inside, extra, 0.0)) * scale
+            for parity in range(2):
+                out_ref[:, parity, line, at] = value[parity * 8 : parity * 8 + 8]
 
 
 def per_device(traces, trace_cell, pattern, fold):
@@ -338,14 +363,14 @@
             pltpu.VMEM((16 * rows, bins), f32),
             pltpu.VMEM((bins, GROUP * records), bf16),
             pltpu.VMEM((16 * rows, GROUP * records), bf16),
-            pltpu.VMEM((4, 2 * rows, bins), f32),
+            pltpu.VMEM((2, 4, 2 * rows, bins // 2), f32),
             dma((5 + NX,)),
             pltpu.SemaphoreType.REGULAR,
             dma((2, 2)),
             dma((2, 2)),
             dma((1,)),
             dma((N_BIN // GROUP + 1,)),
-            dma((2, 2)),
+            dma((2, 4)),
         ],
         compiler_params=pltpu.CompilerParams(
             collective_id=0, has_side_effects=True, vmem_limit_bytes=63 << 20

time: 48.8 us -> 47.1 us (0.965)
  Pallas kernels: 47 us -> 45.3 us
    pallas_call x1, Pallas kernels: 47 us -> 45.3 us  [per_device(): pl.pallas_call(kernel, out_shape=jax.ShapeDtypeStruct((rows // 2, 2, line...]
where the time goes in v4:
time: 47.1 us; the launch traced here: 46.9 us
  Pallas kernels  45.3 us (96%)
  local copies, waits for them, and re-layouts  1.67 us (4%)
    pallas_call x1, Pallas kernels, per_device(): pl.pallas_call(kernel, out_shape=jax.ShapeDtypeStruct((rows // 2, 2, line...  45.3 us
    unnamed x1, local copies, waits for them, and re-layouts  1.67 us

profile of v4, /device:TPU:1, one launch (start us, length us, event | category | flops | bytes accessed | tf_op | source)
XLA Modules:
  0.0 46.9 jit_solution(11817067464759739865)
XLA Ops:
  0.0 45.3 %shard_map.64 = f32[8,2,4,1024]{3,2,1,0:T(4,128)} custom-call(f32[256,1024]{1,0:T(8,128)} %bitcast.2, s32[1,256]{1,0:T(1,128)} %cell_hbm.1, s32[1,256]{1,0:T(1,128)} %pattern_hbm.1, s32[4,16]{1,0:T(4,128)} %fold_hbm.1, bf16[4,2,256,512]{3,2,1,0:T(8,128)(2,1)} %constant.4.clone.table_hbm, f32[8,128]{1,0:T(8,128)} %constant.5.clone.sinc_hbm), custom_call_target="tpu_custom_call" | custom-call | tf_op jit(solution)/shard_map/pallas_call | solution.py:346
  45.3 1.7 %copy.8 = f32[16,4,1024]{2,1,0:T(4,128)} copy(f32[16,4,1024]{2,1,0:T(4,128)} %bitcast.3) | data formatting | bytes 524288

commit v5 on v4

--- a/solution.py
+++ b/solution.py
@@ -61,13 +61,13 @@
 
 
 X_ORDER = (0, 2, 1, 3)
-OWN = NZ * NC - NC
+OWN = 0
 
 
 def offsets(k):
     i, d, e = k // (NZ * NC), k // NC % NZ, k % NC
     along_x = jnp.where(i == 1, X_ORDER[1], jnp.where(i == 2, X_ORDER[2], i))
-    along_z = NZ // 2 + jnp.where(d % 2 == 1, -((d + 1) // 2), d // 2)
+    along_z = jnp.where(d % 2 == 1, (d + 1) // 2, (NZ - d // 2) % NZ)
     return along_x, along_z, e
 
 
@@ -177,7 +177,7 @@
         return carry
 
     transform(0)
-    for d in range(NZ - 1):
+    for d in range(1, NZ):
         start(d * NC)
     pltpu.make_async_copy(spec.at[me], recv.at[OWN], recv_sem.at[unit_of(OWN)]).start()
     pl.semaphore_wait(entered, columns - 1)

time: 47.1 us -> 45.4 us (0.964)
  Pallas kernels: 45.3 us -> 43.6 us
    pallas_call x1, Pallas kernels: 45.3 us -> 43.6 us  [per_device(): pl.pallas_call(kernel, out_shape=jax.ShapeDtypeStruct((rows // 2, 2, line...]
where the time goes in v5:
time: 45.4 us; the launch traced here: 45.3 us
  Pallas kernels  43.6 us (96%)
  local copies, waits for them, and re-layouts  1.67 us (4%)
    pallas_call x1, Pallas kernels, per_device(): pl.pallas_call(kernel, out_shape=jax.ShapeDtypeStruct((rows // 2, 2, line...  43.6 us
    unnamed x1, local copies, waits for them, and re-layouts  1.67 us

profile of v5, /device:TPU:1, one launch (start us, length us, event | category | flops | bytes accessed | tf_op | source)
XLA Modules:
  0.0 45.3 jit_solution(16534733054425840016)
XLA Ops:
  0.0 43.6 %shard_map.64 = f32[8,2,4,1024]{3,2,1,0:T(4,128)} custom-call(f32[256,1024]{1,0:T(8,128)} %bitcast.2, s32[1,256]{1,0:T(1,128)} %cell_hbm.1, s32[1,256]{1,0:T(1,128)} %pattern_hbm.1, s32[4,16]{1,0:T(4,128)} %fold_hbm.1, bf16[4,2,256,512]{3,2,1,0:T(8,128)(2,1)} %constant.4.clone.table_hbm, f32[8,128]{1,0:T(8,128)} %constant.5.clone.sinc_hbm), custom_call_target="tpu_custom_call" | custom-call | tf_op jit(solution)/shard_map/pallas_call | solution.py:346
  43.6 1.7 %copy.8 = f32[16,4,1024]{2,1,0:T(4,128)} copy(f32[16,4,1024]{2,1,0:T(4,128)} %bitcast.3) | data formatting | bytes 524288

commit v6 on v5

--- a/solution.py
+++ b/solution.py
@@ -183,12 +183,14 @@
     pl.semaphore_wait(entered, columns - 1)
     for d in range(NZ):
         start(d * NC + 1)
+    transform(1)
+    lax.fori_loop(NZ * NC, 2 * NZ * NC, start_one, 0)
     wait_for(meta.at[0, pl.ds(1, NZ - 1)], meta_sem.at[0, 1])
     copies(meta, columns, across, meta_sem.at[1])
     wait_for(folds.at[pl.ds(1, NZ - 1)], fold_sem.at[0, 1])
     fold_sum[0] = jnp.sum(folds[...], axis=0)
     copies(fold_sum, columns, across, fold_sem.at[1])
-    for i in range(1, NX):
+    for i in range(2, NX):
         transform(i)
         lax.fori_loop(i * NZ * NC, (i + 1) * NZ * NC, start_one, 0)
 

time: 45.4 us -> 44 us (0.969)
  Pallas kernels: 43.6 us -> 42.2 us
    pallas_call x1, Pallas kernels: 43.6 us -> 42.2 us  [per_device(): pl.pallas_call(kernel, out_shape=jax.ShapeDtypeStruct((rows // 2, 2, line...]
where the time goes in v6:
time: 44 us; the launch traced here: 43.9 us
  Pallas kernels  42.2 us (96%)
  local copies, waits for them, and re-layouts  1.67 us (4%)
    pallas_call x1, Pallas kernels, per_device(): pl.pallas_call(kernel, out_shape=jax.ShapeDtypeStruct((rows // 2, 2, line...  42.2 us
    unnamed x1, local copies, waits for them, and re-layouts  1.67 us

profile of v6, /device:TPU:1, one launch (start us, length us, event | category | flops | bytes accessed | tf_op | source)
XLA Modules:
  0.0 43.9 jit_solution(10614283579120298672)
XLA Ops:
  0.0 42.2 %shard_map.64 = f32[8,2,4,1024]{3,2,1,0:T(4,128)} custom-call(f32[256,1024]{1,0:T(8,128)} %bitcast.2, s32[1,256]{1,0:T(1,128)} %cell_hbm.1, s32[1,256]{1,0:T(1,128)} %pattern_hbm.1, s32[4,16]{1,0:T(4,128)} %fold_hbm.1, bf16[4,2,256,512]{3,2,1,0:T(8,128)(2,1)} %constant.4.clone.table_hbm, f32[8,128]{1,0:T(8,128)} %constant.5.clone.sinc_hbm), custom_call_target="tpu_custom_call" | custom-call | tf_op jit(solution)/shard_map/pallas_call | solution.py:348
  42.2 1.7 %copy.8 = f32[16,4,1024]{2,1,0:T(4,128)} copy(f32[16,4,1024]{2,1,0:T(4,128)} %bitcast.3) | data formatting | bytes 524288
